TPU v7x, 128 devices: a whole 4x4x4 slice. The times are simulated.
128 devices in a mesh: ctx: 16 (over x_lo, z, core), tp: 8 (over y, x_hi).
Axes of the slice: x: 4 (x_hi: 2, x_lo: 2; x = x_hi * 2 + x_lo), y: 4, z: 4, core: 2. Of those that a mesh axis runs over, the one named last changes fastest.
Arguments:
- tokens: bfloat16 [16384, 1024], P(('ctx', 'tp')), may hold values from -6 to 6
- block_table: int32 [16, 2], replicated, may hold values from 0 to 31, as said below
- doc_ids: int32 [4, 4096], replicated, may hold values from 0 to 3, never falling along the last dimension, each value on 1 to 2048 neighbouring positions
- attn_gain: bfloat16 [1024], P('ctx'), may hold values from 0.25 to 1.75
- w_query: bfloat16 [1024, 2048], P('ctx', 'tp'), may hold values from -0.1875 to 0.1875
- w_key: bfloat16 [1024, 1024], P('ctx', 'tp'), may hold values from -0.1875 to 0.1875
- w_value: bfloat16 [1024, 1024], P('ctx', 'tp'), may hold values from -0.1875 to 0.1875
- query_gain: bfloat16 [128], P('ctx'), may hold values from 0.25 to 1.75
- key_gain: bfloat16 [128], P('ctx'), may hold values from 0.25 to 1.75
- w_out: bfloat16 [2048, 1024], P('tp', 'ctx'), may hold values from -1 to 1
- ffn_gain: bfloat16 [1024], P('ctx'), may hold values from 0.25 to 1.75
- w_gate: bfloat16 [1024, 3072], P('ctx', 'tp'), may hold values from -0.1875 to 0.1875
- w_up: bfloat16 [1024, 3072], P('ctx', 'tp'), may hold values from -0.1875 to 0.1875
- w_down: bfloat16 [3072, 1024], P('tp', 'ctx'), may hold values from -0.109375 to 0.109375
- out_grad: bfloat16 [16384, 1024], P(('ctx', 'tp')), may hold values from -6 to 6
Outputs:
- out: bfloat16 [16384, 1024], P(('ctx', 'tp'))
- grad_x: bfloat16 [16384, 1024], P(('ctx', 'tp'))
- grad_attn_gain: float32 [1024], P('ctx')
- grad_w_query: float32 [1024, 2048], P('ctx', 'tp')
- grad_w_key: float32 [1024, 1024], P('ctx', 'tp')
- grad_w_value: float32 [1024, 1024], P('ctx', 'tp')
- grad_query_gain: float32 [128], P('ctx')
- grad_key_gain: float32 [128], P('ctx')
- grad_w_out: float32 [2048, 1024], P('tp', 'ctx')
- grad_ffn_gain: float32 [1024], P('ctx')
- grad_w_gate: float32 [1024, 3072], P('ctx', 'tp')
- grad_w_up: float32 [1024, 3072], P('ctx', 'tp')
- grad_w_down: float32 [3072, 1024], P('tp', 'ctx')
Inputs may be any that keep to these rules, and one draw needn't show every extreme that they name: `block_table`: row c holds a block b below 16 and its mirror 2 * 16 - 1 - b; the first entries of the rows form a permutation, so every block appears once. `doc_ids`: never falling along a row; each document has 1 to 2048 positions, one exactly that many.
All inputs are finite; a program needn't handle non-finite values.
Results may differ from a plain program's by a relative error of at most 0.025.
Values may be sent and summed in bfloat16 or wider, within the bound.
No kernel may reach another device: no remote copies, remote signals or barrier semaphores. Data moves between devices by JAX's collectives and lax.ppermute only.
A program may use at most 192 MiB of HBM per device.

v0:
```python
import math
import jax
import jax.numpy as jnp
from jax import lax
from jax.sharding import PartitionSpec as P

HD = 128
EPS = 1e-06
THETA = 1000000.0
NEG_SCORE = -1e30


def split_up(shard, dim, length):
    before, after = (shard.shape[:dim], shard.shape[dim + 1 :])
    return jnp.moveaxis(shard.reshape(*before, length, -1, *after), dim, 0)


def sent_and_summed(shard, axis, dim):
    parts = split_up(shard, dim, lax.axis_size(axis))
    arrived = lax.all_to_all(parts, axis, split_axis=0, concat_axis=0, tiled=True)
    return arrived.astype(jnp.float32).sum(axis=0)


def normed(values, norm_gain):
    return values * lax.rsqrt(jnp.mean(values * values, axis=-1, keepdims=True) + EPS) * norm_gain


def rotate(values, cos_table, sin_table):
    half_width = values.shape[-1] // 2
    turned = jnp.concatenate([-values[..., half_width:], values[..., :half_width]], axis=-1)
    return values * cos_table + turned * sin_table


def contract_last(left_side, right_side):
    return lax.dot_general(
        left_side, right_side, (((1,), (1,)), ((), ())), preferred_element_type=jnp.float32
    )


def contract_first(left_side, right_side):
    return lax.dot_general(
        left_side, right_side, (((0,), (0,)), ((), ())), preferred_element_type=jnp.float32
    )


def send_grads(stacked):
    return lax.psum_scatter(
        stacked.astype(jnp.bfloat16), "ctx", scatter_dimension=0, tiled=True
    ).astype(jnp.float32)


def per_device(
    tokens,
    block_table,
    doc_ids,
    attn_gain,
    w_query,
    w_key,
    w_value,
    query_gain,
    key_gain,
    w_out,
    ffn_gain,
    w_gate,
    w_up,
    w_down,
    out_grad,
):
    ctx_count = lax.axis_size("ctx")
    tp_count = lax.axis_size("tp")
    ctx_rank = lax.axis_index("ctx")
    rows_dev = tokens.shape[0]
    local_rows = rows_dev * tp_count
    seq_count = doc_ids.shape[0]
    pair_rows = local_rows // seq_count
    seq_keys = pair_rows * ctx_count
    q_heads = w_query.shape[1] // HD
    kv_heads = w_key.shape[1] // HD
    group_size = q_heads // kv_heads
    q_width = q_heads * HD
    k_width = kv_heads * HD
    ff_local = w_gate.shape[1]
    score_scale = HD ** (-0.5)
    key_block = math.gcd(seq_keys, 512)
    key_blocks = seq_keys // key_block
    seq_len = doc_ids.shape[1]
    half_block = pair_rows // 2
    seq_index = jnp.arange(seq_len, dtype=jnp.int32)
    change = jnp.concatenate(
        [jnp.ones((seq_count, 1), dtype=bool), doc_ids[:, 1:] != doc_ids[:, :-1]], axis=1
    )
    doc_starts = lax.cummax(jnp.where(change, seq_index[None, :], 0), axis=1)
    key_index = jnp.arange(seq_keys, dtype=jnp.int32)
    key_inner = key_index % pair_rows
    key_place = (
        block_table[key_index // pair_rows, key_inner // half_block] * half_block
        + key_inner % half_block
    )
    key_doc = doc_ids[:, key_place]
    query_index = jnp.arange(local_rows, dtype=jnp.int32)
    query_seq = query_index // pair_rows
    query_inner = query_index % pair_rows
    query_place = (
        block_table[jnp.zeros_like(query_index) + ctx_rank, query_inner // half_block] * half_block
        + query_inner % half_block
    )
    query_doc = doc_ids[query_seq, query_place]
    query_pos = query_place - doc_starts[query_seq, query_place]
    query_place_s = query_place.reshape(seq_count, pair_rows)
    query_doc_s = query_doc.reshape(seq_count, pair_rows)
    freq_steps = jnp.arange(HD // 2, dtype=jnp.float32) * (2.0 / HD)
    angles = (
        query_pos.astype(jnp.float32)[:, None] * jnp.power(jnp.float32(THETA), -freq_steps)[None, :]
    )
    angles = jnp.concatenate([angles, angles], axis=1)[:, None, :]
    cos_table = jnp.cos(angles)
    sin_table = jnp.sin(angles)
    gain_attn, gain_query, gain_key, w_qkv, w_proj = (
        lax.all_gather(attn_gain, "ctx", axis=0, tiled=True),
        lax.all_gather(query_gain, "ctx", axis=0, tiled=True),
        lax.all_gather(key_gain, "ctx", axis=0, tiled=True),
        lax.all_gather(
            jnp.concatenate([w_query, w_key, w_value], axis=1), "ctx", axis=0, tiled=True
        ),
        lax.all_gather(w_out, "ctx", axis=1, tiled=True),
    )
    tokens_f = tokens.astype(jnp.float32)
    normal_one_f, norm_one_back = jax.vjp(normed, tokens_f, gain_attn.astype(jnp.float32))
    normal_one = normal_one_f.astype(jnp.bfloat16)
    rows_one = lax.all_gather(normal_one, "tp", axis=0, tiled=True)
    projected = jnp.dot(rows_one, w_qkv, preferred_element_type=jnp.float32)
    query_pre = projected[:, :q_width].reshape(local_rows, q_heads, HD)
    key_pre = projected[:, q_width : q_width + k_width].reshape(local_rows, kv_heads, HD)
    value_low = projected[:, q_width + k_width :].astype(jnp.bfloat16)

    def head_prep(pre_values, norm_gain):
        return rotate(normed(pre_values, norm_gain), cos_table, sin_table)

    query_rot, query_back = jax.vjp(head_prep, query_pre, gain_query.astype(jnp.float32))
    key_rot, key_back = jax.vjp(head_prep, key_pre, gain_key.astype(jnp.float32))
    query_low = query_rot.astype(jnp.bfloat16).reshape(
        seq_count, pair_rows, kv_heads, group_size, HD
    )
    key_low = key_rot.astype(jnp.bfloat16).reshape(seq_count, pair_rows, k_width)
    own_values = value_low.reshape(seq_count, pair_rows, k_width)
    keys_all, values_all = (
        lax.all_gather(key_low, "ctx", axis=1, tiled=True),
        lax.all_gather(own_values, "ctx", axis=1, tiled=True),
    )
    keys_seq = keys_all.reshape(seq_count, seq_keys, kv_heads, HD)
    values_seq = values_all.reshape(seq_count, seq_keys, kv_heads, HD)

    def tile_at(start):
        key_tile = lax.dynamic_slice_in_dim(keys_seq, start, key_block, 1)
        value_tile = lax.dynamic_slice_in_dim(values_seq, start, key_block, 1)
        place_tile = lax.dynamic_slice_in_dim(key_place, start, key_block, 0)
        doc_tile = lax.dynamic_slice_in_dim(key_doc, start, key_block, 1)
        scores = (
            jnp.einsum("sqhgd,skhd->shgqk", query_low, key_tile, preferred_element_type=jnp.float32)
            * score_scale
        )
        allowed = (doc_tile[:, None, :] == query_doc_s[:, :, None]) & (
            place_tile[None, None, :] <= query_place_s[:, :, None]
        )
        return (key_tile, value_tile, scores, allowed[:, None, None, :, :])

    starts = jnp.arange(key_blocks, dtype=jnp.int32) * key_block

    def stats_step(running, start):
        peak_score, row_total = running
        key_tile, value_tile, scores, allowed = tile_at(start)
        scores = jnp.where(allowed, scores, NEG_SCORE)
        new_peak = jnp.maximum(peak_score, jnp.max(scores, axis=-1))
        weights = jnp.where(allowed, jnp.exp(scores - new_peak[..., None]), 0.0)
        row_total = row_total * jnp.exp(peak_score - new_peak) + jnp.sum(weights, axis=-1)
        return ((new_peak, row_total), None)

    stat_shape = (seq_count, kv_heads, group_size, pair_rows)
    stats_final = lax.scan(
        stats_step,
        (jnp.full(stat_shape, NEG_SCORE, jnp.float32), jnp.zeros(stat_shape, jnp.float32)),
        starts,
    )[0]
    log_total = stats_final[0] + jnp.log(stats_final[1])

    def output_step(accum, start):
        key_tile, value_tile, scores, allowed = tile_at(start)
        probs_low = jnp.where(allowed, jnp.exp(scores - log_total[..., None]), 0.0).astype(
            jnp.bfloat16
        )
        return (
            accum
            + jnp.einsum(
                "shgqk,skhd->sqhgd", probs_low, value_tile, preferred_element_type=jnp.float32
            ),
            None,
        )

    head_shape = (seq_count, pair_rows, kv_heads, group_size, HD)
    attended = lax.scan(output_step, jnp.zeros(head_shape, jnp.float32), starts)[0]
    attn_low = attended.reshape(local_rows, q_width).astype(jnp.bfloat16)
    resid = tokens_f + lax.psum_scatter(
        jnp.dot(attn_low, w_proj, preferred_element_type=jnp.float32).astype(jnp.bfloat16),
        "tp",
        scatter_dimension=0,
        tiled=True,
    ).astype(jnp.float32)
    gain_ffn, w_gu, w_dn = (
        lax.all_gather(ffn_gain, "ctx", axis=0, tiled=True),
        lax.all_gather(jnp.concatenate([w_gate, w_up], axis=1), "ctx", axis=0, tiled=True),
        lax.all_gather(w_down, "ctx", axis=1, tiled=True),
    )
    normal_two_f, norm_two_back = jax.vjp(normed, resid, gain_ffn.astype(jnp.float32))
    normal_two = normal_two_f.astype(jnp.bfloat16)
    rows_two = lax.all_gather(normal_two, "tp", axis=0, tiled=True)
    gate_up = jnp.dot(rows_two, w_gu, preferred_element_type=jnp.float32)
    gate = gate_up[:, :ff_local]
    up_proj = gate_up[:, ff_local:]
    sigmoid_gate = jax.nn.sigmoid(gate)
    silu_gate = gate * sigmoid_gate
    hidden = (silu_gate * up_proj).astype(jnp.bfloat16)
    out = (
        resid
        + sent_and_summed(
            jnp.dot(hidden, w_dn, preferred_element_type=jnp.float32).astype(jnp.bfloat16), "tp", 0
        )
    ).astype(jnp.bfloat16)
    grad_rows = lax.all_gather(out_grad, "tp", axis=0, tiled=True)
    grad_hidden = contract_last(grad_rows, w_dn)
    grad_gate = grad_hidden * up_proj * (sigmoid_gate * (1.0 + gate * (1.0 - sigmoid_gate)))
    grad_up = grad_hidden * silu_gate
    grad_gu = jnp.concatenate([grad_gate, grad_up], axis=1).astype(jnp.bfloat16)
    mlp_grads = jnp.concatenate(
        [contract_first(rows_two, grad_gu), contract_first(grad_rows, hidden)], axis=1
    )
    mlp_early = send_grads(mlp_grads)
    grad_norm_two = sent_and_summed(contract_last(grad_gu, w_gu).astype(jnp.bfloat16), "tp", 0)
    grad_resid_norm, grad_gain_ffn = norm_two_back(grad_norm_two)
    grad_resid = out_grad.astype(jnp.float32) + grad_resid_norm
    branch_rows = lax.all_gather(grad_resid.astype(jnp.bfloat16), "tp", axis=0, tiled=True)
    grad_attn_low = contract_last(branch_rows, w_proj).astype(jnp.bfloat16)
    grad_out_cols = contract_first(branch_rows, attn_low)
    grad_attn_heads = grad_attn_low.reshape(head_shape)
    delta = jnp.transpose(
        jnp.sum(grad_attn_heads.astype(jnp.float32) * attended, axis=-1), (0, 2, 3, 1)
    )

    def scores_grad(probs, grad_probs, delta_here):
        return (probs * (grad_probs - delta_here[..., None])).astype(jnp.bfloat16)

    def grad_step(carry, start):
        accum, key_grad_all, value_grad_all = carry
        key_tile, value_tile, scores, allowed = tile_at(start)
        probs = jnp.where(allowed, jnp.exp(scores - log_total[..., None]), 0.0)
        probs_low = probs.astype(jnp.bfloat16)
        grad_value = jnp.einsum(
            "shgqk,sqhgd->skhd", probs_low, grad_attn_heads, preferred_element_type=jnp.float32
        )
        grad_probs = jnp.einsum(
            "sqhgd,skhd->shgqk", grad_attn_heads, value_tile, preferred_element_type=jnp.float32
        )
        grad_scores = scores_grad(probs, grad_probs, delta)
        accum = (
            accum
            + jnp.einsum(
                "shgqk,skhd->sqhgd", grad_scores, key_tile, preferred_element_type=jnp.float32
            )
            * score_scale
        )
        grad_key = (
            jnp.einsum(
                "shgqk,sqhgd->skhd", grad_scores, query_low, preferred_element_type=jnp.float32
            )
            * score_scale
        )
        key_grad_all = lax.dynamic_update_slice_in_dim(
            key_grad_all, grad_key.reshape(seq_count, key_block, k_width), start, 1
        )
        value_grad_all = lax.dynamic_update_slice_in_dim(
            value_grad_all, grad_value.reshape(seq_count, key_block, k_width), start, 1
        )
        return ((accum, key_grad_all, value_grad_all), None)

    kv_zero = jnp.zeros((seq_count, seq_keys, k_width), jnp.float32)
    grad_query, key_grad_all, value_grad_all = lax.scan(
        grad_step, (jnp.zeros(head_shape, jnp.float32), kv_zero, kv_zero), starts
    )[0]
    grad_keys, grad_values = (
        lax.psum_scatter(
            key_grad_all.astype(jnp.bfloat16), "ctx", scatter_dimension=1, tiled=True
        ).astype(jnp.float32),
        lax.psum_scatter(
            value_grad_all.astype(jnp.bfloat16), "ctx", scatter_dimension=1, tiled=True
        ).astype(jnp.float32),
    )
    grad_query_pre, grad_gain_query = query_back(grad_query.reshape(local_rows, q_heads, HD))
    grad_key_pre, grad_gain_key = key_back(grad_keys.reshape(local_rows, kv_heads, HD))
    grad_qkv = jnp.concatenate(
        [
            grad_query_pre.reshape(local_rows, q_width),
            grad_key_pre.reshape(local_rows, k_width),
            grad_values.reshape(local_rows, k_width),
        ],
        axis=1,
    ).astype(jnp.bfloat16)
    attn_grads = jnp.concatenate([contract_first(rows_one, grad_qkv), grad_out_cols], axis=1)
    grad_norm_one = sent_and_summed(contract_last(grad_qkv, w_qkv).astype(jnp.bfloat16), "tp", 0)
    grad_input_norm, grad_gain_attn = norm_one_back(grad_norm_one)
    grad_x = (grad_resid + grad_input_norm).astype(jnp.bfloat16)
    gain_sums = lax.psum(
        (grad_gain_attn, grad_gain_query, grad_gain_key, grad_gain_ffn), ("ctx", "tp")
    )
    d_share = gain_sums[0].shape[0] // ctx_count
    h_share = gain_sums[1].shape[0] // ctx_count
    attn_owned = send_grads(attn_grads)
    return (
        out,
        grad_x,
        lax.dynamic_slice_in_dim(gain_sums[0], ctx_rank * d_share, d_share),
        attn_owned[:, :q_width],
        attn_owned[:, q_width : q_width + k_width],
        attn_owned[:, q_width + k_width : q_width + 2 * k_width],
        lax.dynamic_slice_in_dim(gain_sums[1], ctx_rank * h_share, h_share),
        lax.dynamic_slice_in_dim(gain_sums[2], ctx_rank * h_share, h_share),
        jnp.transpose(attn_owned[:, q_width + 2 * k_width :]),
        lax.dynamic_slice_in_dim(gain_sums[3], ctx_rank * d_share, d_share),
        mlp_early[:, :ff_local],
        mlp_early[:, ff_local : 2 * ff_local],
        jnp.transpose(mlp_early[:, 2 * ff_local :]),
    )


def solution(mesh):
    in_specs = (
        P(("ctx", "tp"), None),
        P(),
        P(),
        P("ctx"),
        P("ctx", "tp"),
        P("ctx", "tp"),
        P("ctx", "tp"),
        P("ctx"),
        P("ctx"),
        P("tp", "ctx"),
        P("ctx"),
        P("ctx", "tp"),
        P("ctx", "tp"),
        P("tp", "ctx"),
        P(("ctx", "tp"), None),
    )
    out_specs = (
        P(("ctx", "tp"), None),
        P(("ctx", "tp"), None),
        P("ctx"),
        P("ctx", "tp"),
        P("ctx", "tp"),
        P("ctx", "tp"),
        P("ctx"),
        P("ctx"),
        P("tp", "ctx"),
        P("ctx"),
        P("ctx", "tp"),
        P("ctx", "tp"),
        P("tp", "ctx"),
    )
    return jax.shard_map(
        per_device, mesh=mesh, in_specs=in_specs, out_specs=out_specs, check_vma=False
    )
```

profile of v0, /device:TPU:1, one launch (start us, length us, event | category | flops | bytes accessed | tf_op | source)
XLA Modules:
  0.0 1124.1 jit_solution(7905820449707120170)
XLA Ops:
  14.7 30.3 %all-reduce.11 = (bf16[1024]{0:T(1024)(128)(2,1)S(1)}, bf16[128]{0:T(256)(128)(2,1)S(1)}, bf16[128]{0:T(256)(128)(2,1)S(1)}, bf16[1024]{0:T(1024)(128)(2,1)}) all-reduce(bf16[1024]{0:T(1024)(128)(2,1)S(1)} %dynamic-update-slice, bf16[128]{0:T(256)(128)(2,1)S(1)} %dynamic-update-slice.1, ...), channel_id=1, replica_groups=mesh['ctx'=16,'tp'=8] {'ctx'}, use_global_device_ids=true, to_apply=%add.6 | all-reduce | flops 2304 | bytes 9216
  52.0 8.8 gather_fusion.2
  60.9 9.1 gather_fusion.4
  70.9 33.8 %all-gather.9.cloned.1.call-done = bf16[1024,1024]{1,0:T(8,128)(2,1)} async-done(((bf16[128,1024]{1,0:T(8,128)(2,1)}), bf16[1024,1024]{1,0:T(8,128)(2,1)}) %all-gather.9.cloned.1.call-update) | async-done | bytes 2097168 | tf_op jit(solution)/shard_map/all_gather | solution.py:130
  112.1 9.1 gather_fusion.3
  124.0 33.8 %gather_fusion = s32[4096]{0:T(1024)S(1)} fusion(s32[16,2]{0,1:T(2,128)S(1)} %copy-done, s32[4096]{0:T(1024)S(1)} %bitcast.382), kind=kCustom, calls=%fused_computation | custom fusion | bytes 65536 | tf_op jit(solution)/shard_map/gather | solution.py:96
  157.9 15.8 %gather_fusion.1 = s32[4096,4]{1,0:T(8,128)} fusion(s32[4,4096]{0,1:T(8,128)} %copy.155, s32[4096]{0:T(1024)S(1)} %broadcast_clamp_fusion), kind=kCustom, calls=%fused_computation.1 | custom fusion | bytes 147456 | tf_op jit(solution)/shard_map/gather | solution.py:99
  181.5 22.6 %all_gather.49 = bf16[256,1024]{0,1:T(8,128)(2,1)} all-gather(bf16[256,64]{0,1:T(8,128)(2,1)S(1)} %copy-done.40), channel_id=1, replica_groups=mesh['ctx'=16,'tp'=8] {'ctx'}, dimensions={1}, use_global_device_ids=true | all-gather | bytes 557056 | tf_op jit(solution)/shard_map/all_gather | solution.py:125
  213.8 56.3 %while.42 = (s32[]{:T(128)}, f32[4,1,2,256]{3,2,0,1:T(2,128)S(1)}, f32[4,1,2,256]{3,2,0,1:T(2,128)S(1)}, s32[8]{0:T(128)}, s32[4,4096]{1,0:T(4,128)S(1)}, /*inde...) while((s32[]{:T(128)}, f32[4,1,2,256]{3,2,0,1:T(2,128)S(1)}, ...), condition=%wide.wide.region_8.9_spmd.clone, body=%wide.wide.region_5.8_spmd.clone.sunk | while | flops 278407168 | bytes 11155674 | solution.py:179
  270.2 54.3 %while.43 = (s32[]{:T(128)}, f32[4,256,1,2,128]{1,4,3,0,2:T(8,128)S(1)}, s32[8]{0:T(128)}, bf16[4,4096,1,128]{3,1,0,2:T(8,128)(2,1)}, s32[4,4096]{1,0:T(4,128)S(...) while((s32[]{:T(128)}, ...), condition=%wide.wide.region_10.11_spmd.clone, body=%wide.wide.region_9.10_spmd.clone.sunk | while | flops 543162368 | bytes 4767452 | solution.py:200
  328.5 68.6 %reduce-scatter.10.cloned.1.call-done = bf16[128,1024]{1,0:T(8,128)(2,1)} async-done(((bf16[1024,1024]{1,0:T(8,128)(2,1)}), bf16[128,1024]{1,0:T(8,128)(2,1)}) %reduce-scatter.10.cloned.1.call-update) | async-done | bytes 262160 | tf_op jit(solution)/shard_map/reduce_scatter | solution.py:202
  400.8 23.9 %all_gather.53 = bf16[384,1024]{0,1:T(8,128)(2,1)S(1)} all-gather(bf16[384,64]{0,1:T(8,128)(2,1)} %param.34), channel_id=1, replica_groups=mesh['ctx'=16,'tp'=8] {'ctx'}, dimensions={1}, use_global_device_ids=true | all-gather | bytes 835584 | tf_op jit(solution)/shard_map/all_gather | solution.py:211
  424.7 9.1 all-gather.19.cloned.1.call-done
  433.8 55.7 %all-gather.17.cloned.1.call-done = bf16[1024,1024]{1,0:T(8,128)(2,1)} async-done(((bf16[128,1024]{1,0:T(8,128)(2,1)}), bf16[1024,1024]{1,0:T(8,128)(2,1)}) %all-gather.17.cloned.1.call-update) | async-done | bytes 2097168 | tf_op jit(solution)/shard_map/all_gather | solution.py:215
  495.0 48.6 %all-gather.21.cloned.1.call-done = bf16[1024,1024]{1,0:T(8,128)(2,1)} async-done(((bf16[128,1024]{1,0:T(8,128)(2,1)}), bf16[1024,1024]{1,0:T(8,128)(2,1)}) %all-gather.21.cloned.1.call-update) | async-done | bytes 2097168 | tf_op jit(solution)/shard_map/all_gather | solution.py:228
  550.7 30.0 %all_to_all.15 = bf16[8,128,1024]{2,1,0:T(8,128)(2,1)S(1)} all-to-all(bf16[8,128,1024]{2,1,0:T(8,128)(2,1)S(1)} %bitcast.393), channel_id=1, replica_groups=mesh['ctx'=16,'tp'=8] {'tp'}, dimensions={0} | all-to-all | bytes 4194304 | tf_op jit(solution)/shard_map/all_to_all | solution.py:20
  583.5 52.6 %all-gather.23.cloned.1.call-done = bf16[1024,1024]{1,0:T(8,128)(2,1)} async-done(((bf16[128,1024]{1,0:T(8,128)(2,1)}), bf16[1024,1024]{1,0:T(8,128)(2,1)}) %all-gather.23.cloned.1.call-update) | async-done | bytes 2097168 | tf_op jit(solution)/shard_map/all_gather | solution.py:240
  648.6 176.8 %while.44 = (s32[]{:T(128)}, f32[4,256,1,2,128]{1,4,3,0,2:T(8,128)S(1)}, bf16[4,4096,128]{2,1,0:T(8,128)(2,1)}, bf16[4,4096,128]{2,1,0:T(8,128)(2,1)}, s32[8]{0:...) while((s32[]{:T(128)}, ...), condition=%wide.wide.region_18.19_spmd.clone, body=%wide.wide.region_17.18_spmd.clone.sunk | while | flops 1355546624 | bytes 29423888 | solution.py:285
  659.7 5.6 dynamic_update_slice.12
  854.6 41.9 %reduce-scatter.14.cloned.1.call-done = bf16[4,256,128]{2,1,0:T(8,128)(2,1)} async-done(((bf16[4,4096,128]{2,1,0:T(8,128)(2,1)}), bf16[4,256,128]{2,1,0:T(8,128)(2,1)}) %reduce-scatter.14.cloned.1.call-update) | async-done | bytes 262160 | tf_op jit(solution)/shard_map/reduce_scatter | solution.py:292
  897.6 64.9 %reduce-scatter.12.cloned.1.call-done = bf16[4,256,128]{2,1,0:T(8,128)(2,1)} async-done(((bf16[4,4096,128]{2,1,0:T(8,128)(2,1)}), bf16[4,256,128]{2,1,0:T(8,128)(2,1)}) %reduce-scatter.12.cloned.1.call-update) | async-done | bytes 262160 | tf_op jit(solution)/shard_map/reduce_scatter | solution.py:289
  976.5 6.8 all-to-all-start.2
  986.1 45.8 %reduce-scatter.18.cloned.1.call-done = bf16[64,1152]{1,0:T(8,128)(2,1)} async-done(((bf16[1024,1152]{1,0:T(8,128)(2,1)}), bf16[64,1152]{1,0:T(8,128)(2,1)}) %reduce-scatter.18.cloned.1.call-update) | async-done | bytes 147472
  1040.3 68.1 %all-reduce.10 = (f32[1024]{0:T(1024)S(1)}, f32[128]{0:T(128)S(1)}, f32[128]{0:T(128)S(1)}, f32[1024]{0:T(1024)S(1)}) all-reduce(f32[1024]{0:T(1024)S(1)} %get-tuple-element.576, f32[128]{0:T(128)S(1)} %get-tuple-element.574, f32[128]{0:T(128)S(1)} %get-tuple-element.570, ...), channel_id=1, replica_groups=mesh['ctx'=16,'tp'=8] {'ctx','tp'}, use_global_device_ids=true, to_apply=%region_26.27 | all-reduce | flops 2304 | bytes 18432 | tf_op jit(solution)/shard_map/psum | solution.py:310
  (501 shorter events, 374.6 us)
Async XLA Ops:
  7.2 63.7 %all-gather.11.cloned.1.call-start = ((), (), s32[]{:S(2)}) async-start(), calls=%async_computation.9 | async-start | bytes 1114112 | tf_op jit(solution)/shard_map/all_gather | solution.py:122
  8.7 96.0 %all-gather.9.cloned.1.call-start = ((), (), s32[]{:S(2)}) async-start(), calls=%async_computation.8 | async-start | bytes 2359296 | tf_op jit(solution)/shard_map/all_gather | solution.py:130
  49.0 164.8 %all-gather.15.cloned.1.call-start = ((), (), s32[]{:S(2)}) async-start(), calls=%async_computation.11 | async-start | bytes 4456448 | tf_op jit(solution)/shard_map/all_gather | solution.py:147
  107.8 99.0 %copy-start.3 = (f32[1024,512]{0,1:T(8,128)}, f32[1024,512]{0,1:T(8,128)S(1)}, u32[]{:S(2)}) copy-start(f32[1024,512]{0,1:T(8,128)S(1)} %fusion.161) | copy-start | bytes 6291460
  112.0 158.2 %all-gather.13.cloned.1.call-start = ((), (), s32[]{:S(2)}) async-start(), calls=%async_computation.10 | async-start | bytes 4456448 | tf_op jit(solution)/shard_map/all_gather | solution.py:148
  213.6 183.5 %reduce-scatter.10.cloned.1.call-start = ((), (), s32[]{:S(2)}) async-start(), calls=%async_computation.12 | async-start | bytes 2359296 | tf_op jit(solution)/shard_map/reduce_scatter | solution.py:202
  325.5 71.5 %copy-start.5 = (bf16[128,1024]{1,0:T(8,128)(2,1)S(1)}, bf16[128,1024]{1,0:T(8,128)(2,1)}, u32[]{:S(2)}) copy-start(bf16[128,1024]{1,0:T(8,128)(2,1)} %param.21) | copy-start | bytes 786436
  327.7 106.2 %all-gather.19.cloned.1.call-start = ((), (), s32[]{:S(2)}) async-start(), calls=%async_computation.14 | async-start | bytes 1671168 | tf_op jit(solution)/shard_map/all_gather | solution.py:210
  328.4 161.1 %all-gather.17.cloned.1.call-start = ((), (), s32[]{:S(2)}) async-start(), calls=%async_computation.13 | async-start | bytes 2359296 | tf_op jit(solution)/shard_map/all_gather | solution.py:215
  400.0 143.7 %all-gather.21.cloned.1.call-start = ((), (), s32[]{:S(2)}) async-start(), calls=%async_computation.15 | async-start | bytes 2359296 | tf_op jit(solution)/shard_map/all_gather | solution.py:228
  400.7 235.4 %all-gather.23.cloned.1.call-start = ((), (), s32[]{:S(2)}) async-start(), calls=%async_computation.16 | async-start | bytes 2359296 | tf_op jit(solution)/shard_map/all_gather | solution.py:240
  424.7 118.9 %copy-start.24 = (bf16[384,1024]{0,1:T(8,128)(2,1)}, bf16[384,1024]{0,1:T(8,128)(2,1)S(1)}, u32[]{:S(2)}) copy-start(bf16[384,1024]{0,1:T(8,128)(2,1)S(1)} %all_gather.53) | copy-start | bytes 2359300
  583.4 313.1 %reduce-scatter.14.cloned.1.call-start = ((), (), s32[]{:S(2)}) async-start(), calls=%async_computation.18 | async-start | bytes 4456448 | tf_op jit(solution)/shard_map/reduce_scatter | solution.py:292
  825.5 137.0 %reduce-scatter.12.cloned.1.call-start = ((), (), s32[]{:S(2)}) async-start(), calls=%async_computation.17 | async-start | bytes 4456448 | tf_op jit(solution)/shard_map/reduce_scatter | solution.py:289
  826.2 205.7 %reduce-scatter.18.cloned.1.call-start = ((), (), s32[]{:S(2)}) async-start(), calls=%async_computation.20 | async-start | bytes 2506752
  841.1 135.5 %all-to-all-start = ((bf16[8,128,1024]{2,1,0:T(8,128)(2,1)}), bf16[8,128,1024]{2,1,0:T(8,128)(2,1)}, u32[]{:S(2)}, u32[]{:S(2)}) async-start(bf16[8,128,1024]{2,1,0:T(8,128)(2,1)} %bitcast.391), calls=%async_computation.1 | async-start | bytes 4194304 | tf_op jit(solution)/shard_map/all_to_all | solution.py:20
  845.4 267.7 %reduce-scatter.16.cloned.1.call-start = ((), (), s32[]{:S(2)}) async-start(), calls=%async_computation.19 | async-start | bytes 1671168
  854.6 110.9 %copy-start.15 = (f32[1024,1,64]{0,2,1:T(8,128)S(1)}, f32[1024,1,64]{0,2,1:T(8,128)}, u32[]{:S(2)}) copy-start(f32[1024,1,64]{0,2,1:T(8,128)} %get-tuple-element.686) | copy-start | bytes 786436
  976.5 62.4 %all-to-all-start.2 = ((bf16[8,128,1024]{2,1,0:T(8,128)(2,1)}), bf16[8,128,1024]{2,1,0:T(8,128)(2,1)S(1)}, u32[]{:S(2)}, u32[]{:S(2)}) async-start(bf16[8,128,1024]{2,1,0:T(8,128)(2,1)} %bitcast.392), calls=%async_computation.5 | async-start | bytes 4194304 | tf_op jit(solution)/shard_map/all_to_all | solution.py:20
  1035.5 75.2 %copy-start.51 = (f32[128]{0:T(128)S(1)}, f32[128]{0:T(128)}, u32[]{:S(2)}) copy-start(f32[128]{0:T(128)} %copy-done.50) | copy-start | bytes 1540
  1035.5 75.2 %copy-start.9 = (f32[128,1024]{1,0:T(8,128)S(1)}, f32[128,1024]{1,0:T(8,128)}, u32[]{:S(2)}) copy-start(f32[128,1024]{1,0:T(8,128)} %copy-done.8) | copy-start | bytes 1572868
  1035.5 75.2 %copy-start.11 = (bf16[128,1024]{1,0:T(8,128)(2,1)S(1)}, bf16[128,1024]{1,0:T(8,128)(2,1)}, u32[]{:S(2)}) copy-start(bf16[128,1024]{1,0:T(8,128)(2,1)} %reduce-scatter.10.cloned.1.call-done) | copy-start | bytes 786436
  1035.5 75.3 %copy-start.17 = (bf16[128,1024]{1,0:T(8,128)(2,1)S(1)}, bf16[128,1024]{1,0:T(8,128)(2,1)}, u32[]{:S(2)}) copy-start(bf16[128,1024]{1,0:T(8,128)(2,1)} %param.35) | copy-start | bytes 786436
  1035.5 75.3 %copy-start.48 = (f32[128]{0:T(128)S(1)}, f32[128]{0:T(128)}, u32[]{:S(2)}) copy-start(f32[128]{0:T(128)} %copy-done.47) | copy-start | bytes 1540
  (53 other events, 509.5 us)
Sparse Core Ops, SparseCore 0:
  10.3 36.2 all-gather.10
  49.5 55.1 all-gather.8
  112.1 36.1 all-gather.14
  213.7 33.6 all-gather.12
  327.8 69.2 reduce-scatter.9
  399.2 34.5 all-gather.18
  436.7 52.7 all-gather.16
  491.9 51.7 all-gather.20
  583.5 52.5 all-gather.22
  825.6 70.8 reduce-scatter.13
  898.9 63.5 reduce-scatter.11
  964.7 67.1 reduce-scatter.17
  1034.3 60.6 reduce-scatter.15
where the time goes:
time: 1140 us; the launch traced here: 1120 us
  waiting for transfers between devices  423 us (37%)
  local copies, waits for them, and re-layouts  248 us (22%)
  blocking collectives  175 us (15%)
  matrix products  135 us (12%)
  other arithmetic  66.5 us (6%)
  loops' own time  47.7 us (4%)
  between operations  16.8 us (1%)
  starting transfers between devices  12.1 us (1%)
    reduce_scatter x1, waiting for transfers between devices, per_device(): lax.psum_scatter(jnp.dot(attn_low, w_proj, preferred_element_type=jnp.flo...  68.6 us
    psum x1, blocking collectives, per_device(): lax.psum((grad_gain_attn, grad_gain_query, grad_gain_key, grad_gain_ffn),...  68.1 us
    reduce_scatter x1, waiting for transfers between devices, per_device(): lax.psum_scatter(key_grad_all.astype(jnp.bfloat16), 'ctx', scatter_dimens...  64.9 us
    all_gather x1, waiting for transfers between devices, per_device(): rows_two = lax.all_gather(normal_two, 'tp', axis=0, tiled=True)  55.7 us
    all_gather x1, waiting for transfers between devices, per_device(): lax.all_gather(grad_resid.astype(jnp.bfloat16), 'tp', axis=0, tiled=True)  52.6 us
    all_gather x1, waiting for transfers between devices, per_device(): grad_rows = lax.all_gather(out_grad, 'tp', axis=0, tiled=True)  48.6 us
    unnamed x15, waiting for transfers between devices  47.4 us
    dynamic_update_slice x8, local copies, waits for them, and re-layouts, grad_step(): lax.dynamic_update_slice_in_dim(key_grad_all, grad_key.reshape(seq_count,...  43.9 us
  transfers between devices with their start and end apart: 15, of which 9 were waited for; matrix products, arithmetic and copies ran while one was open for 18% of the time, Pallas kernels for 0%

commit v1 on v0

--- a/solution.py
+++ b/solution.py
@@ -8,6 +8,13 @@
 EPS = 1e-06
 THETA = 1000000.0
 NEG_SCORE = -1e30
+
+
+def all_by_exchange(x, axis, d):
+    size = lax.axis_size(axis)
+    parts = jnp.stack([x for _ in range(size)])
+    parts = lax.all_to_all(parts, axis, split_axis=0, concat_axis=0)
+    return jnp.concatenate(parts, axis=d)
 
 
 def split_up(shard, dim, length):
@@ -225,7 +232,7 @@
             jnp.dot(hidden, w_dn, preferred_element_type=jnp.float32).astype(jnp.bfloat16), "tp", 0
         )
     ).astype(jnp.bfloat16)
-    grad_rows = lax.all_gather(out_grad, "tp", axis=0, tiled=True)
+    grad_rows = all_by_exchange(out_grad, "tp", 0)
     grad_hidden = contract_last(grad_rows, w_dn)
     grad_gate = grad_hidden * up_proj * (sigmoid_gate * (1.0 + gate * (1.0 - sigmoid_gate)))
     grad_up = grad_hidden * silu_gate

time: 1140 us -> 1090 us (0.956)
  waiting for transfers between devices: 423 us -> 346 us
  blocking collectives: 175 us -> 199 us
    all_gather x1 -> x0, waiting for transfers between devices: 48.6 us -> none  [per_device(): grad_rows = lax.all_gather(out_grad, 'tp', axis=0, tiled=True)]
    all_gather x1, blocking collectives: 23.9 us -> 47.5 us  [per_device(): lax.all_gather(w_down, 'ctx', axis=1, tiled=True)]
    all_gather x1, waiting for transfers between devices: 55.7 us -> 37.2 us  [per_device(): rows_two = lax.all_gather(normal_two, 'tp', axis=0, tiled=True)]
    unnamed x15 -> x14, waiting for transfers between devices: 47.4 us -> 46.7 us
  transfers between devices with their start and end apart: 15 -> 15, of which waited for: 9 -> 7; matrix products, arithmetic and copies ran while one was open for 18% -> 19% of each run, Pallas kernels for 0% -> 0%
where the time goes in v1:
time: 1090 us; the launch traced here: 1080 us
  waiting for transfers between devices  346 us (32%)
  local copies, waits for them, and re-layouts  249 us (23%)
  blocking collectives  199 us (18%)
  matrix products  135 us (12%)
  other arithmetic  66.5 us (6%)
  loops' own time  47.7 us (4%)
  between operations  17.2 us (2%)
  starting transfers between devices  16.4 us (2%)
    reduce_scatter x1, waiting for transfers between devices, per_device(): lax.psum_scatter(jnp.dot(attn_low, w_proj, preferred_element_type=jnp.flo...  68.6 us
    psum x1, blocking collectives, per_device(): lax.psum((grad_gain_attn, grad_gain_query, grad_gain_key, grad_gain_ffn),...  68.3 us
    reduce_scatter x1, waiting for transfers between devices, per_device(): lax.psum_scatter(key_grad_all.astype(jnp.bfloat16), 'ctx', scatter_dimens...  64.7 us
    all_gather x1, waiting for transfers between devices, per_device(): lax.all_gather(grad_resid.astype(jnp.bfloat16), 'tp', axis=0, tiled=True)  52.6 us
    all_gather x1, blocking collectives, per_device(): lax.all_gather(w_down, 'ctx', axis=1, tiled=True)  47.5 us
    unnamed x14, waiting for transfers between devices  46.7 us
    dynamic_update_slice x8, local copies, waits for them, and re-layouts, grad_step(): lax.dynamic_update_slice_in_dim(key_grad_all, grad_key.reshape(seq_count,...  43.8 us
    dynamic_update_slice x8, local copies, waits for them, and re-layouts, grad_step(): lax.dynamic_update_slice_in_dim(value_grad_all, grad_value.reshape(seq_co...  43.7 us
  transfers between devices with their start and end apart: 15, of which 7 were waited for; matrix products, arithmetic and copies ran while one was open for 19% of the time, Pallas kernels for 0%

profile of v1, /device:TPU:1, one launch (start us, length us, event | category | flops | bytes accessed | tf_op | source)
XLA Modules:
  0.0 1076.9 jit_solution(12098484189925053266)
XLA Ops:
  14.7 30.3 %all-reduce.11 = (bf16[1024]{0:T(1024)(128)(2,1)S(1)}, bf16[128]{0:T(256)(128)(2,1)S(1)}, bf16[128]{0:T(256)(128)(2,1)S(1)}, bf16[1024]{0:T(1024)(128)(2,1)}) all-reduce(bf16[1024]{0:T(1024)(128)(2,1)S(1)} %dynamic-update-slice, bf16[128]{0:T(256)(128)(2,1)S(1)} %dynamic-update-slice.1, ...), channel_id=1, replica_groups=mesh['ctx'=16,'tp'=8] {'ctx'}, use_global_device_ids=true, to_apply=%add.6 | all-reduce | flops 2304 | bytes 9216
  52.0 8.8 gather_fusion.2
  60.9 9.1 gather_fusion.4
  70.9 33.8 %all-gather.8.cloned.1.call-done = bf16[1024,1024]{1,0:T(8,128)(2,1)} async-done(((bf16[128,1024]{1,0:T(8,128)(2,1)}), bf16[1024,1024]{1,0:T(8,128)(2,1)}) %all-gather.8.cloned.1.call-update) | async-done | bytes 2097168 | tf_op jit(solution)/shard_map/all_gather | solution.py:137
  112.1 9.1 gather_fusion.3
  124.0 33.8 %gather_fusion = s32[4096]{0:T(1024)S(1)} fusion(s32[16,2]{0,1:T(2,128)S(1)} %copy-done, s32[4096]{0:T(1024)S(1)} %bitcast.383), kind=kCustom, calls=%fused_computation | custom fusion | bytes 65536 | tf_op jit(solution)/shard_map/gather | solution.py:103
  157.9 15.7 %gather_fusion.1 = s32[4096,4]{1,0:T(8,128)} fusion(s32[4,4096]{0,1:T(8,128)} %copy.155, s32[4096]{0:T(1024)S(1)} %broadcast_clamp_fusion), kind=kCustom, calls=%fused_computation.1 | custom fusion | bytes 147456 | tf_op jit(solution)/shard_map/gather | solution.py:106
  181.4 22.6 %all_gather.46 = bf16[256,1024]{0,1:T(8,128)(2,1)} all-gather(bf16[256,64]{0,1:T(8,128)(2,1)S(1)} %copy-done.40), channel_id=1, replica_groups=mesh['ctx'=16,'tp'=8] {'ctx'}, dimensions={1}, use_global_device_ids=true | all-gather | bytes 557056 | tf_op jit(solution)/shard_map/all_gather | solution.py:132
  213.7 56.3 %while.42 = (s32[]{:T(128)}, f32[4,1,2,256]{3,2,0,1:T(2,128)S(1)}, f32[4,1,2,256]{3,2,0,1:T(2,128)S(1)}, s32[8]{0:T(128)}, s32[4,4096]{1,0:T(4,128)S(1)}, /*inde...) while((s32[]{:T(128)}, f32[4,1,2,256]{3,2,0,1:T(2,128)S(1)}, ...), condition=%wide.wide.region_8.9_spmd.clone, body=%wide.wide.region_5.8_spmd.clone.sunk | while | flops 278407168 | bytes 11155674 | solution.py:186
  270.0 54.3 %while.43 = (s32[]{:T(128)}, f32[4,256,1,2,128]{1,4,3,0,2:T(8,128)S(1)}, s32[8]{0:T(128)}, bf16[4,4096,1,128]{3,1,0,2:T(8,128)(2,1)}, s32[4,4096]{1,0:T(4,128)S(...) while((s32[]{:T(128)}, ...), condition=%wide.wide.region_10.11_spmd.clone, body=%wide.wide.region_9.10_spmd.clone.sunk | while | flops 543162368 | bytes 4767452 | solution.py:207
  328.3 68.6 %reduce-scatter.10.cloned.1.call-done = bf16[128,1024]{1,0:T(8,128)(2,1)} async-done(((bf16[1024,1024]{1,0:T(8,128)(2,1)}), bf16[128,1024]{1,0:T(8,128)(2,1)}) %reduce-scatter.10.cloned.1.call-update) | async-done | bytes 262160 | tf_op jit(solution)/shard_map/reduce_scatter | solution.py:209
  406.0 47.5 %all_gather.50 = bf16[384,1024]{0,1:T(8,128)(2,1)S(1)} all-gather(bf16[384,64]{0,1:T(8,128)(2,1)} %param.34), channel_id=1, replica_groups=mesh['ctx'=16,'tp'=8] {'ctx'}, dimensions={1}, use_global_device_ids=true | all-gather | bytes 835584 | tf_op jit(solution)/shard_map/all_gather | solution.py:218
  453.5 37.2 %all-gather.16.cloned.1.call-done = bf16[1024,1024]{1,0:T(8,128)(2,1)} async-done(((bf16[128,1024]{1,0:T(8,128)(2,1)}), bf16[1024,1024]{1,0:T(8,128)(2,1)}) %all-gather.16.cloned.1.call-update) | async-done | bytes 2097168 | tf_op jit(solution)/shard_map/all_gather | solution.py:222
  503.3 30.0 %all_to_all.20 = bf16[8,128,1024]{2,1,0:T(8,128)(2,1)S(1)} all-to-all(bf16[8,128,1024]{2,1,0:T(8,128)(2,1)S(1)} %bitcast.394), channel_id=1, replica_groups=mesh['ctx'=16,'tp'=8] {'tp'}, dimensions={0} | all-to-all | bytes 4194304 | tf_op jit(solution)/shard_map/all_to_all | solution.py:27
  536.0 52.6 %all-gather.20.cloned.1.call-done = bf16[1024,1024]{1,0:T(8,128)(2,1)} async-done(((bf16[128,1024]{1,0:T(8,128)(2,1)}), bf16[1024,1024]{1,0:T(8,128)(2,1)}) %all-gather.20.cloned.1.call-update) | async-done | bytes 2097168 | tf_op jit(solution)/shard_map/all_gather | solution.py:247
  601.1 176.6 %while.44 = (s32[]{:T(128)}, f32[4,256,1,2,128]{1,4,3,0,2:T(8,128)S(1)}, bf16[4,4096,128]{2,1,0:T(8,128)(2,1)}, bf16[4,4096,128]{2,1,0:T(8,128)(2,1)}, s32[8]{0:...) while((s32[]{:T(128)}, ...), condition=%wide.wide.region_18.19_spmd.clone, body=%wide.wide.region_17.18_spmd.clone.sunk | while | flops 1355546624 | bytes 29423888 | solution.py:292
  612.3 5.6 dynamic_update_slice.12
  679.0 5.6 dynamic_update_slice.12
  745.7 5.6 dynamic_update_slice.12
  806.8 41.9 %reduce-scatter.14.cloned.1.call-done = bf16[4,256,128]{2,1,0:T(8,128)(2,1)} async-done(((bf16[4,4096,128]{2,1,0:T(8,128)(2,1)}), bf16[4,256,128]{2,1,0:T(8,128)(2,1)}) %reduce-scatter.14.cloned.1.call-update) | async-done | bytes 262160 | tf_op jit(solution)/shard_map/reduce_scatter | solution.py:299
  849.8 64.7 %reduce-scatter.12.cloned.1.call-done = bf16[4,256,128]{2,1,0:T(8,128)(2,1)} async-done(((bf16[4,4096,128]{2,1,0:T(8,128)(2,1)}), bf16[4,256,128]{2,1,0:T(8,128)(2,1)}) %reduce-scatter.12.cloned.1.call-update) | async-done | bytes 262160 | tf_op jit(solution)/shard_map/reduce_scatter | solution.py:296
  928.6 6.8 all-to-all-start.3
  938.1 46.0 %reduce-scatter.18.cloned.1.call-done = bf16[64,1152]{1,0:T(8,128)(2,1)} async-done(((bf16[1024,1152]{1,0:T(8,128)(2,1)}), bf16[64,1152]{1,0:T(8,128)(2,1)}) %reduce-scatter.18.cloned.1.call-update) | async-done | bytes 147472
  992.5 68.3 %all-reduce.10 = (f32[1024]{0:T(1024)S(1)}, f32[128]{0:T(128)S(1)}, f32[128]{0:T(128)S(1)}, f32[1024]{0:T(1024)S(1)}) all-reduce(f32[1024]{0:T(1024)S(1)} %get-tuple-element.576, f32[128]{0:T(128)S(1)} %get-tuple-element.574, f32[128]{0:T(128)S(1)} %get-tuple-element.570, ...), channel_id=1, replica_groups=mesh['ctx'=16,'tp'=8] {'ctx','tp'}, use_global_device_ids=true, to_apply=%region_26.27 | all-reduce | flops 2304 | bytes 18432 | tf_op jit(solution)/shard_map/psum | solution.py:317
  (501 shorter events, 368.4 us)
Async XLA Ops:
  7.2 63.7 %all-gather.10.cloned.1.call-start = ((), (), s32[]{:S(2)}) async-start(), calls=%async_computation.10 | async-start | bytes 1114112 | tf_op jit(solution)/shard_map/all_gather | solution.py:129
  8.7 96.0 %all-gather.8.cloned.1.call-start = ((), (), s32[]{:S(2)}) async-start(), calls=%async_computation.9 | async-start | bytes 2359296 | tf_op jit(solution)/shard_map/all_gather | solution.py:137
  49.0 164.7 %all-gather.14.cloned.1.call-start = ((), (), s32[]{:S(2)}) async-start(), calls=%async_computation.12 | async-start | bytes 4456448 | tf_op jit(solution)/shard_map/all_gather | solution.py:154
  107.8 98.9 %copy-start.3 = (f32[1024,512]{0,1:T(8,128)}, f32[1024,512]{0,1:T(8,128)S(1)}, u32[]{:S(2)}) copy-start(f32[1024,512]{0,1:T(8,128)S(1)} %fusion.161) | copy-start | bytes 6291460
  112.0 158.0 %all-gather.12.cloned.1.call-start = ((), (), s32[]{:S(2)}) async-start(), calls=%async_computation.11 | async-start | bytes 4456448 | tf_op jit(solution)/shard_map/all_gather | solution.py:155
  213.4 183.5 %reduce-scatter.10.cloned.1.call-start = ((), (), s32[]{:S(2)}) async-start(), calls=%async_computation.13 | async-start | bytes 2359296 | tf_op jit(solution)/shard_map/reduce_scatter | solution.py:209
  325.4 71.6 %copy-start.5 = (bf16[128,1024]{1,0:T(8,128)(2,1)S(1)}, bf16[128,1024]{1,0:T(8,128)(2,1)}, u32[]{:S(2)}) copy-start(bf16[128,1024]{1,0:T(8,128)(2,1)} %param.21) | copy-start | bytes 786436
  327.5 72.4 %copy-start.16 = (bf16[128,1024]{1,0:T(8,128)(2,1)S(1)}, bf16[128,1024]{1,0:T(8,128)(2,1)}, u32[]{:S(2)}) copy-start(bf16[128,1024]{1,0:T(8,128)(2,1)} %param.35) | copy-start | bytes 786436
  327.5 126.0 %all-gather.18.cloned.1.call-start = ((), (), s32[]{:S(2)}) async-start(), calls=%async_computation.15 | async-start | bytes 1671168 | tf_op jit(solution)/shard_map/all_gather | solution.py:217
  328.3 162.5 %all-gather.16.cloned.1.call-start = ((), (), s32[]{:S(2)}) async-start(), calls=%async_computation.14 | async-start | bytes 2359296 | tf_op jit(solution)/shard_map/all_gather | solution.py:222
  401.6 94.7 %all-to-all-start.1 = ((bf16[8,128,1024]{2,1,0:T(8,128)(2,1)}), bf16[8,128,1024]{2,1,0:T(8,128)(2,1)}, u32[]{:S(2)}, u32[]{:S(2)}) async-start(bf16[8,128,1024]{2,1,0:T(8,128)(2,1)} %stack.2), calls=%async_computation.2 | async-start | bytes 4194304 | tf_op jit(solution)/shard_map/all_to_all | solution.py:16
  405.9 182.8 %all-gather.20.cloned.1.call-start = ((), (), s32[]{:S(2)}) async-start(), calls=%async_computation.16 | async-start | bytes 2359296 | tf_op jit(solution)/shard_map/all_gather | solution.py:247
  535.9 312.8 %reduce-scatter.14.cloned.1.call-start = ((), (), s32[]{:S(2)}) async-start(), calls=%async_computation.18 | async-start | bytes 4456448 | tf_op jit(solution)/shard_map/reduce_scatter | solution.py:299
  777.8 136.7 %reduce-scatter.12.cloned.1.call-start = ((), (), s32[]{:S(2)}) async-start(), calls=%async_computation.17 | async-start | bytes 4456448 | tf_op jit(solution)/shard_map/reduce_scatter | solution.py:296
  778.4 205.8 %reduce-scatter.18.cloned.1.call-start = ((), (), s32[]{:S(2)}) async-start(), calls=%async_computation.20 | async-start | bytes 2506752
  793.3 135.2 %all-to-all-start = ((bf16[8,128,1024]{2,1,0:T(8,128)(2,1)}), bf16[8,128,1024]{2,1,0:T(8,128)(2,1)}, u32[]{:S(2)}, u32[]{:S(2)}) async-start(bf16[8,128,1024]{2,1,0:T(8,128)(2,1)} %bitcast.392), calls=%async_computation.1 | async-start | bytes 4194304 | tf_op jit(solution)/shard_map/all_to_all | solution.py:27
  797.7 267.9 %reduce-scatter.16.cloned.1.call-start = ((), (), s32[]{:S(2)}) async-start(), calls=%async_computation.19 | async-start | bytes 1671168
  806.8 110.7 %copy-start.15 = (f32[1024,1,64]{0,2,1:T(8,128)S(1)}, f32[1024,1,64]{0,2,1:T(8,128)}, u32[]{:S(2)}) copy-start(f32[1024,1,64]{0,2,1:T(8,128)} %get-tuple-element.686) | copy-start | bytes 786436
  928.6 62.6 %all-to-all-start.3 = ((bf16[8,128,1024]{2,1,0:T(8,128)(2,1)}), bf16[8,128,1024]{2,1,0:T(8,128)(2,1)S(1)}, u32[]{:S(2)}, u32[]{:S(2)}) async-start(bf16[8,128,1024]{2,1,0:T(8,128)(2,1)} %bitcast.393), calls=%async_computation.6 | async-start | bytes 4194304 | tf_op jit(solution)/shard_map/all_to_all | solution.py:27
  987.7 75.5 %copy-start.51 = (f32[128]{0:T(128)S(1)}, f32[128]{0:T(128)}, u32[]{:S(2)}) copy-start(f32[128]{0:T(128)} %copy-done.50) | copy-start | bytes 1540
  987.7 75.5 %copy-start.9 = (f32[128,1024]{1,0:T(8,128)S(1)}, f32[128,1024]{1,0:T(8,128)}, u32[]{:S(2)}) copy-start(f32[128,1024]{1,0:T(8,128)} %copy-done.8) | copy-start | bytes 1572868
  987.7 75.5 %copy-start.11 = (bf16[128,1024]{1,0:T(8,128)(2,1)S(1)}, bf16[128,1024]{1,0:T(8,128)(2,1)}, u32[]{:S(2)}) copy-start(bf16[128,1024]{1,0:T(8,128)(2,1)} %reduce-scatter.10.cloned.1.call-done) | copy-start | bytes 786436
  987.7 75.5 %copy-start.17 = (bf16[128,1024]{1,0:T(8,128)(2,1)S(1)}, bf16[128,1024]{1,0:T(8,128)(2,1)}, u32[]{:S(2)}) copy-start(bf16[128,1024]{1,0:T(8,128)(2,1)} %param.35) | copy-start | bytes 786436
  987.7 75.5 %copy-start.48 = (f32[128]{0:T(128)S(1)}, f32[128]{0:T(128)}, u32[]{:S(2)}) copy-start(f32[128]{0:T(128)} %copy-done.47) | copy-start | bytes 1540
  (53 other events, 550.1 us)
Sparse Core Ops, SparseCore 0:
  10.3 36.2 all-gather.9
  49.5 55.1 all-gather.7
  112.2 36.1 all-gather.13
  213.5 33.6 all-gather.11
  327.6 69.2 reduce-scatter.9
  399.1 36.0 all-gather.17
  438.1 52.5 all-gather.15
  536.1 52.5 all-gather.19
  777.9 70.7 reduce-scatter.13
  851.0 63.4 reduce-scatter.11
  916.9 67.2 reduce-scatter.17
  986.4 60.6 reduce-scatter.15
